TPU v7x, 32 devices: a whole 2x2x4 slice. The times are simulated.
32 devices in a mesh: dp: 4 (over y, x), mp: 8 (over z, core).
Axes of the slice: x: 2, y: 2, z: 4, core: 2. Of those that a mesh axis runs over, the one named last changes fastest.
Arguments:
- activations: bfloat16 [4096, 2048], P('dp', 'mp'), may hold values from -6 to 6
- out_grad: bfloat16 [4096, 8192], P('dp'), may hold values from -0.8984375 to 0.8984375
- old_weight: bfloat16 [8, 256, 8192], P('mp', 'dp'), may hold values from -0.125 to 0.125
- old_first: float32 [8, 256, 8192], P('mp', 'dp'), may hold values from -6 to 6
- old_second: float32 [8, 256, 8192], P('mp', 'dp'), may hold values from 0.25 to 4
- step: int32 [1], replicated, may hold values from 1 to 31
- next_input: bfloat16 [4096, 2048], P('dp', 'mp'), may hold values from -6 to 6
Outputs:
- new_weight: bfloat16 [8, 344, 8192], P('mp', 'dp')
- new_first: float32 [8, 344, 8192], P('mp', 'dp')
- new_second: float32 [8, 344, 8192], P('mp', 'dp')
- output: bfloat16 [4096, 8192], P('dp', 'mp')
Inputs may be any that keep to these rules, and one draw needn't show every extreme that they name: `step`: the number of Adam steps taken, this one included.
All inputs are finite; a program needn't handle non-finite values.
Results may differ from a plain program's by a relative error of at most 0.0049.
Values may be sent and summed in bfloat16 or wider, within the bound.
A program may use at most 192 MiB of HBM per device.

v0:
```python
import jax
import jax.numpy as jnp
from jax import lax
from jax.sharding import PartitionSpec as P


def partner(i, k, n):
    return i ^ k if n & n - 1 == 0 else (i + k) % n


def exchange(block, axis, k):
    n = lax.axis_size(axis)
    return lax.ppermute(block, axis, [(i, partner(i, k, n)) for i in range(n)])


def target(k, n, axis):
    me = lax.axis_index(axis)
    return me ^ k if n & n - 1 == 0 else lax.rem(me + k, n)


def to_front(block, axis):
    n = lax.axis_size(axis)
    return lax.ppermute(block, axis, [(i, i - 1) for i in range(1, n)])


def body(activations, out_grad, old_weight, old_first, old_second, step, next_input):
    owners = lax.axis_size("dp")
    owner = lax.axis_index("dp")
    old_rows = old_weight.shape[1]
    width = old_weight.shape[2]
    held_rows = old_rows * owners
    shard_rows = (held_rows + owners - 2) // (owners - 1)
    input_all = lax.all_gather(next_input, "mp", axis=1, tiled=True)
    part = lax.dot_general(
        activations, out_grad, (((0,), (0,)), ((), ())), preferred_element_type=jnp.float32
    ).astype(jnp.bfloat16)
    part = part.reshape(owners, old_rows, width)
    grad = lax.dynamic_index_in_dim(part, owner, 0, keepdims=False).astype(jnp.float32)
    for k in range(1, owners):
        away = lax.dynamic_index_in_dim(part, target(k, owners, "dp"), 0, keepdims=False)
        grad = grad + exchange(away, "dp", k).astype(jnp.float32)
    step_float = step[0].astype(jnp.float32)
    first_fix = 1.0 - jnp.power(jnp.float32(0.9), step_float)
    second_fix = 1.0 - jnp.power(jnp.float32(0.95), step_float)
    new_first = 0.9 * old_first[0] + 0.1 * grad
    new_second = 0.95 * old_second[0] + 0.05 * grad * grad
    update = new_first / first_fix / (jnp.sqrt(new_second / second_fix) + 1e-08)
    new_weight = (old_weight[0].astype(jnp.float32) - 0.01 * update).astype(jnp.bfloat16)
    weight_part = lax.all_to_all(new_weight, "mp", split_axis=1, concat_axis=0, tiled=True)
    heads = lax.axis_size("mp")
    weight_part = weight_part.reshape(heads, old_rows, -1)
    weight_cols = lax.all_gather(weight_part, "dp", axis=1, tiled=True)
    weight_cols = weight_cols.reshape(heads * held_rows, -1)
    begin = owner * (shard_rows - old_rows)

    def mine(block):
        behind = to_front(block.astype(jnp.bfloat16), "dp").astype(block.dtype)
        rows = jnp.concatenate([block, behind, jnp.zeros((shard_rows, width), block.dtype)], 0)
        return lax.dynamic_slice_in_dim(rows, begin, shard_rows, 0)[None]

    outs = (mine(new_weight), mine(new_first), mine(new_second))
    output = jnp.dot(input_all, weight_cols, preferred_element_type=jnp.float32).astype(
        jnp.bfloat16
    )
    return (*outs, output)


def solution(mesh):
    return jax.shard_map(
        body,
        mesh=mesh,
        in_specs=(
            P("dp", "mp"),
            P("dp", None),
            P("mp", "dp", None),
            P("mp", "dp", None),
            P("mp", "dp", None),
            P(),
            P("dp", "mp"),
        ),
        out_specs=(P("mp", "dp", None), P("mp", "dp", None), P("mp", "dp", None), P("dp", "mp")),
        check_vma=False,
    )
```

profile of v0, /device:TPU:0, one launch (start us, length us, event | category | flops | bytes accessed | tf_op | source)
XLA Modules:
  0.0 292.9 jit_solution(17170010049314651664)
XLA Ops:
  8.2 10.7 %convolution_convert_fusion = bf16[256,8192]{1,0:T(8,128)(2,1)S(1)} fusion(bf16[1024,256]{1,0:T(8,128)(2,1)S(1)} %copy-done, bf16[1024,8192]{1,0:T(8,128)(2,1)} %param.8), kind=kOutput, calls=%fused_computation | convolution fusion | flops 4297064448 | bytes 21495808 | tf_op jit(solution)/shard_map/dot_general | solution.py:34
  19.0 1.8 dynamic-slice_bitcast_fusion.2
  21.9 2.9 %collective-permute-start = (bf16[64,8192]{1,0:T(8,128)(2,1)}, bf16[64,8192]{1,0:T(8,128)(2,1)S(1)}, u32[]{:S(2)}, u32[]{:S(2)}) collective-permute-start(bf16[64,8192]{1,0:T(8,128)(2,1)} %get-tuple-element.26), channel_id=1, source_target_pairs={{0,8},{8,0},{16,24},{24,16},{1,9},{9,1},{17,25},{25,17},{2,10},{10... | collective-permute-start | bytes 3145736 | tf_op jit(solution)/shard_map/ppermute | solution.py:13
  24.8 1.5 collective-permute-start.1
  27.1 21.9 %collective-permute-done = bf16[64,8192]{1,0:T(8,128)(2,1)S(1)} collective-permute-done((bf16[64,8192]{1,0:T(8,128)(2,1)}, bf16[64,8192]{1,0:T(8,128)(2,1)S(1)}, u32[]{:S(2)}, u32[]{:S(2)}) %collective-permute-start) | collective-permute-done | bytes 1048608 | tf_op jit(solution)/shard_map/ppermute | solution.py:13
  49.0 23.1 %collective-permute-done.1 = bf16[64,8192]{1,0:T(8,128)(2,1)S(1)} collective-permute-done((bf16[64,8192]{1,0:T(8,128)(2,1)}, bf16[64,8192]{1,0:T(8,128)(2,1)S(1)}, u32[]{:S(2)}, u32[]{:S(2)}) %collective-permute-start.1) | collective-permute-done | bytes 1048608 | tf_op jit(solution)/shard_map/ppermute | solution.py:13
  73.1 5.9 %fusion.11 = (bf16[64,8192]{1,0:T(8,128)(2,1)}, f32[64,8192]{1,0:T(8,128)S(1)}, bf16[64,8192]{1,0:T(8,128)(2,1)}, f32[64,8192]{1,0:T(8,128)S(1)}) fusion(bf16[64,8192]{1,0:T(8,128)(2,1)} %collective-permute-done.2, bf16[64,8192]{1,0:T(8,128)(2,1)} %copy-done.8, bf16[64,8192]{1,0:T(8,128)(2,1)} %copy-done.7, bf16[4,64,8192]{2,1,0:T(8,128)(2,1)} %bitcast.42, ...), kind=kLoop, calls=%fused_computation.29 | loop fusion | flops 8388608 | bytes 14680068 | tf_op jit(solution)/shard_map/convert_element_type | solution.py:57
  80.4 31.3 %all_to_all.16 = bf16[64,8,1024]{2,0,1:T(8,128)(2,1)S(1)} all-to-all(bf16[64,8,1024]{2,0,1:T(8,128)(2,1)S(1)} %bitcast.46), channel_id=1, replica_groups=mesh['dp'=4,'mp'=8] {'mp'}, dimensions={1} | all-to-all | bytes 2097152 | tf_op jit(solution)/shard_map/all_to_all | solution.py:49
  111.7 1.5 copy.16
  116.8 1.5 collective-permute-start.3
  118.2 35.3 %collective-permute-done.4 = bf16[64,8192]{1,0:T(8,128)(2,1)} collective-permute-done((bf16[64,8192]{1,0:T(8,128)(2,1)}, bf16[64,8192]{1,0:T(8,128)(2,1)}, u32[]{:S(2)}, u32[]{:S(2)}) %collective-permute-start.4) | collective-permute-done | bytes 1048608 | tf_op jit(solution)/shard_map/ppermute | solution.py:23
  153.5 1.4 convert_element_type.60
  154.9 21.1 %collective-permute-done.5 = bf16[64,8192]{1,0:T(8,128)(2,1)} collective-permute-done((bf16[64,8192]{1,0:T(8,128)(2,1)}, bf16[64,8192]{1,0:T(8,128)(2,1)}, u32[]{:S(2)}, u32[]{:S(2)}) %collective-permute-start.5) | collective-permute-done | bytes 1048608 | tf_op jit(solution)/shard_map/ppermute | solution.py:23
  176.0 1.4 convert_element_type.62
  177.4 4.0 %fusion.1 = (f32[86,8192]{1,0:T(8,128)}, f32[86,8192]{1,0:T(8,128)}) fusion(s32[]{:T(128)S(6)} %select_n.22, f32[64,8192]{1,0:T(8,128)S(1)} %get-tuple-element.21, f32[64,8192]{1,0:T(8,128)S(1)} %convert_element_type.62, f32[86]{0:T(128)S(1)} %pad_dynamic-slice_fusion.6, f32[64,8192]{1,0:T(8,128)S(1)} %convert_element_type.60, f32[64,8192]{1,0:T(8,128)S(1)} %copy-done.3), kind=kLoop, calls=%fused_computation.9 | loop fusion | flops 2818048 | bytes 14025052 | tf_op jit(solution)/shard_map/concatenate | solution.py:58
  181.3 6.7 %broadcast_in_dim.14 = f32[1,86,8192]{2,0,1:T(1,128)} reshape(f32[86,8192]{1,0:T(8,128)} %get-tuple-element.30) | data formatting | bytes 5636096 | tf_op jit(solution)/shard_map/broadcast_in_dim | solution.py:59
  188.0 4.7 %broadcast_in_dim.15 = f32[1,86,8192]{2,0,1:T(1,128)} reshape(f32[86,8192]{1,0:T(8,128)S(1)} %copy-done.5) | data formatting | bytes 5636096 | tf_op jit(solution)/shard_map/broadcast_in_dim | solution.py:59
  192.8 4.1 %collective-permute-done.3 = bf16[64,8192]{1,0:T(8,128)(2,1)} collective-permute-done((bf16[64,8192]{1,0:T(8,128)(2,1)}, bf16[64,8192]{1,0:T(8,128)(2,1)}, u32[]{:S(2)}, u32[]{:S(2)}) %collective-permute-start.3) | collective-permute-done | bytes 1048608 | tf_op jit(solution)/shard_map/ppermute | solution.py:23
  196.9 3.4 %fusion.10 = bf16[1,86,8192]{2,1,0:T(8,128)(2,1)} fusion(s32[]{:T(128)S(6)} %select_n.22, bf16[64,8192]{1,0:T(8,128)(2,1)} %copy-done.6, bf16[64,8192]{1,0:T(8,128)(2,1)} %collective-permute-done.3, bf16[86]{0:T(256)(128)(2,1)S(1)} %pad_dynamic-slice_fusion.7), kind=kLoop, calls=%fused_computation.22 | loop fusion | flops 4227072 | bytes 3506352 | tf_op jit(solution)/shard_map/broadcast_in_dim | solution.py:59
  200.3 25.5 %all-gather.3.cloned.1.call-done = bf16[8,256,1024]{2,0,1:T(8,128)(2,1)} async-done(((bf16[8,64,1024]{2,0,1:T(8,128)(2,1)}), bf16[8,256,1024]{2,0,1:T(8,128)(2,1)}) %all-gather.3.cloned.1.call-update) | async-done | bytes 4194320 | tf_op jit(solution)/shard_map/all_gather | solution.py:52
  225.8 6.5 %copy.17 = bf16[8,256,1024]{2,1,0:T(8,128)(2,1)} copy(bf16[8,256,1024]{2,0,1:T(8,128)(2,1)} %all-gather.3.cloned.1.call-done) | data formatting | bytes 8388608 | tf_op jit(solution)/shard_map/all_gather | solution.py:52
  232.3 42.9 %all-gather.5.cloned.1.call-done = bf16[1024,2048]{1,0:T(8,128)(2,1)} async-done(((bf16[1024,256]{1,0:T(8,128)(2,1)}), bf16[1024,2048]{1,0:T(8,128)(2,1)}) %all-gather.5.cloned.1.call-update) | async-done | bytes 4194320 | tf_op jit(solution)/shard_map/all_gather | solution.py:33
  275.2 8.3 %convert_bitcast_fusion = bf16[1024,1024]{0,1:T(8,128)(2,1)S(1)} fusion(bf16[2048,1024]{1,0:T(8,128)(2,1)} %bitcast.44, bf16[1024,2048]{1,0:T(8,128)(2,1)} %all-gather.5.cloned.1.call-done), kind=kOutput, calls=%fused_computation.19 | convolution fusion | flops 4296015872 | bytes 10485760 | tf_op jit(solution)/shard_map/dot_general | solution.py:62
  283.5 2.6 copy.18
  (34 shorter events, 8.1 us)
Async XLA Ops:
  7.2 1.1 copy-start
  7.2 218.6 %all-gather.3.cloned.1.call-start = ((), (), s32[]{:S(2)}) async-start(), calls=%async_computation.1 | async-start | bytes 5242880 | tf_op jit(solution)/shard_map/all_gather | solution.py:52
  19.0 2.9 %copy-start.4 = (bf16[256,8192]{1,0:T(8,128)(2,1)}, bf16[256,8192]{1,0:T(8,128)(2,1)S(1)}, u32[]{:S(2)}) copy-start(bf16[256,8192]{1,0:T(8,128)(2,1)S(1)} %convolution_convert_fusion) | copy-start | bytes 12582916
  21.9 27.1 %collective-permute-start = (bf16[64,8192]{1,0:T(8,128)(2,1)}, bf16[64,8192]{1,0:T(8,128)(2,1)S(1)}, u32[]{:S(2)}, u32[]{:S(2)}) collective-permute-start(bf16[64,8192]{1,0:T(8,128)(2,1)} %get-tuple-element.26), channel_id=1, source_target_pairs={{0,8},{8,0},{16,24},{24,16},{1,9},{9,1},{17,25},{25,17},{2,10},{10... | collective-permute-start | bytes 3145736 | tf_op jit(solution)/shard_map/ppermute | solution.py:13
  24.8 47.3 %collective-permute-start.1 = (bf16[64,8192]{1,0:T(8,128)(2,1)}, bf16[64,8192]{1,0:T(8,128)(2,1)S(1)}, u32[]{:S(2)}, u32[]{:S(2)}) collective-permute-start(bf16[64,8192]{1,0:T(8,128)(2,1)} %get-tuple-element.28), channel_id=1, source_target_pairs={{0,16},{8,24},{16,0},{24,8},{1,17},{9,25},{17,1},{25,9},{2,18},{10... | collective-permute-start | bytes 3145736 | tf_op jit(solution)/shard_map/ppermute | solution.py:13
  26.4 46.8 %collective-permute-start.2 = (bf16[64,8192]{1,0:T(8,128)(2,1)}, bf16[64,8192]{1,0:T(8,128)(2,1)}, u32[]{:S(2)}, u32[]{:S(2)}) collective-permute-start(bf16[64,8192]{1,0:T(8,128)(2,1)} %get-tuple-element.27), channel_id=1, source_target_pairs={{0,24},{8,16},{16,8},{24,0},{1,25},{9,17},{17,9},{25,1},{2,26},{10... | collective-permute-start | bytes 3145736 | tf_op jit(solution)/shard_map/ppermute | solution.py:13
  27.1 51.9 %copy-start.9 = (bf16[1,64,8192]{2,1,0:T(8,128)(2,1)S(1)}, bf16[1,64,8192]{2,1,0:T(8,128)(2,1)}, u32[]{:S(2)}) copy-start(bf16[1,64,8192]{2,1,0:T(8,128)(2,1)} %param.9) | copy-start | bytes 3145732
  49.0 23.1 %copy-start.7 = (bf16[64,8192]{1,0:T(8,128)(2,1)}, bf16[64,8192]{1,0:T(8,128)(2,1)S(1)}, u32[]{:S(2)}) copy-start(bf16[64,8192]{1,0:T(8,128)(2,1)S(1)} %collective-permute-done) | copy-start | bytes 3145732
  72.2 1.0 copy-start.8
  79.0 1.3 copy-start.2
  80.3 31.4 %copy-start.6 = (bf16[64,8192]{1,0:T(8,128)(2,1)}, bf16[64,8192]{1,0:T(8,128)(2,1)S(1)}, u32[]{:S(2)}) copy-start(bf16[64,8192]{1,0:T(8,128)(2,1)S(1)} %fusion.7) | copy-start | bytes 3145732
  113.2 162.0 %all-gather.5.cloned.1.call-start = ((), (), s32[]{:S(2)}) async-start(), calls=%async_computation.2 | async-start | bytes 4718592 | tf_op jit(solution)/shard_map/all_gather | solution.py:33
  114.0 39.5 %collective-permute-start.4 = (bf16[64,8192]{1,0:T(8,128)(2,1)}, bf16[64,8192]{1,0:T(8,128)(2,1)}, u32[]{:S(2)}, u32[]{:S(2)}) collective-permute-start(bf16[64,8192]{1,0:T(8,128)(2,1)} %get-tuple-element.24), channel_id=1, source_target_pairs={{8,0},{16,8},{24,16},{9,1},{17,9},{25,17},{10,2},{18,10},{26,18},{... | collective-permute-start | bytes 3145736 | tf_op jit(solution)/shard_map/ppermute | solution.py:23
  115.3 60.7 %collective-permute-start.5 = (bf16[64,8192]{1,0:T(8,128)(2,1)}, bf16[64,8192]{1,0:T(8,128)(2,1)}, u32[]{:S(2)}, u32[]{:S(2)}) collective-permute-start(bf16[64,8192]{1,0:T(8,128)(2,1)} %get-tuple-element.20), channel_id=1, source_target_pairs={{8,0},{16,8},{24,16},{9,1},{17,9},{25,17},{10,2},{18,10},{26,18},{... | collective-permute-start | bytes 3145736 | tf_op jit(solution)/shard_map/ppermute | solution.py:23
  116.8 80.1 %collective-permute-start.3 = (bf16[64,8192]{1,0:T(8,128)(2,1)}, bf16[64,8192]{1,0:T(8,128)(2,1)}, u32[]{:S(2)}, u32[]{:S(2)}) collective-permute-start(bf16[64,8192]{1,0:T(8,128)(2,1)} %copy-done.6), channel_id=1, source_target_pairs={{8,0},{16,8},{24,16},{9,1},{17,9},{25,17},{10,2},{18,10},{26,18},{... | collective-permute-start | bytes 3145736 | tf_op jit(solution)/shard_map/ppermute | solution.py:23
  154.9 22.5 %copy-start.3 = (f32[64,8192]{1,0:T(8,128)S(1)}, f32[64,8192]{1,0:T(8,128)}, u32[]{:S(2)}) copy-start(f32[64,8192]{1,0:T(8,128)} %copy-done.2) | copy-start | bytes 6291460
  181.3 6.7 %copy-start.5 = (f32[86,8192]{1,0:T(8,128)S(1)}, f32[86,8192]{1,0:T(8,128)}, u32[]{:S(2)}) copy-start(f32[86,8192]{1,0:T(8,128)} %get-tuple-element.29) | copy-start | bytes 8454148
  275.2 10.9 %copy-start.1 = (bf16[1024,256]{1,0:T(8,128)(2,1)S(1)}, bf16[1024,256]{1,0:T(8,128)(2,1)}, u32[]{:S(2)}) copy-start(bf16[1024,256]{1,0:T(8,128)(2,1)} %param.7) | copy-start | bytes 1572868
Sparse Core Ops, SparseCore 0:
  113.3 112.3 all-gather.2
  227.4 47.7 all-gather.4
where the time goes:
time: 293 us
  waiting for transfers between devices  175 us (60%)
  blocking collectives  31.3 us (11%)
  local copies, waits for them, and re-layouts  27.4 us (9%)
  matrix products  19 us (6%)
  other arithmetic  17 us (6%)
  between operations  14.9 us (5%)
  starting transfers between devices  8.58 us (3%)
    ppermute x3, waiting for transfers between devices, to_front(): return lax.ppermute(block, axis, [(i, i - 1) for i in range(1, n)])  60.5 us
    ppermute x3, waiting for transfers between devices, exchange(): return lax.ppermute(block, axis, [(i, partner(i, k, n)) for i in range(n)])  45 us
    all_gather x1, waiting for transfers between devices, body(): input_all = lax.all_gather(next_input, 'mp', axis=1, tiled=True)  42.9 us
    all_to_all x1, blocking collectives, body(): lax.all_to_all(new_weight, 'mp', split_axis=1, concat_axis=0, tiled=True)  31.3 us
    all_gather x1, waiting for transfers between devices, body(): weight_cols = lax.all_gather(weight_part, 'dp', axis=1, tiled=True)  25.5 us
    broadcast_in_dim x2, local copies, waits for them, and re-layouts, mine(): return lax.dynamic_slice_in_dim(rows, begin, shard_rows, 0)[None]  11.4 us
    dot_general x1, matrix products, body(): lax.dot_general(activations, out_grad, (((0,), (0,)), ((), ())), preferre...  10.7 us
    convert_element_type x3, other arithmetic, mine(): behind = to_front(block.astype(jnp.bfloat16), 'dp').astype(block.dtype)  8.57 us
  transfers between devices with their start and end apart: 8, of which 7 were waited for; matrix products, arithmetic and copies ran while one was open for 10% of the time, Pallas kernels for 0%

commit v1 on v0

--- a/solution.py
+++ b/solution.py
@@ -46,7 +46,10 @@
     new_second = 0.95 * old_second[0] + 0.05 * grad * grad
     update = new_first / first_fix / (jnp.sqrt(new_second / second_fix) + 1e-08)
     new_weight = (old_weight[0].astype(jnp.float32) - 0.01 * update).astype(jnp.bfloat16)
-    weight_part = lax.all_to_all(new_weight, "mp", split_axis=1, concat_axis=0, tiled=True)
+    weight_part = jnp.concatenate(
+        lax.all_to_all(jnp.stack(jnp.split(new_weight, lax.axis_size("mp"), axis=1)), "mp", 0, 0),
+        axis=0,
+    )
     heads = lax.axis_size("mp")
     weight_part = weight_part.reshape(heads, old_rows, -1)
     weight_cols = lax.all_gather(weight_part, "dp", axis=1, tiled=True)

time: 293 us -> 245 us (0.84)
  waiting for transfers between devices: 175 us -> 132 us
  local copies, waits for them, and re-layouts: 27.4 us -> 20.9 us
    all_gather x1, waiting for transfers between devices: 42.9 us -> 0.01 us  [body(): input_all = lax.all_gather(next_input, 'mp', axis=1, tiled=True)]
    all_gather x1 -> x0, local copies, waits for them, and re-layouts: 6.49 us -> none  [body(): weight_cols = lax.all_gather(weight_part, 'dp', axis=1, tiled=True)]
    unnamed x21 -> x26, local copies, waits for them, and re-layouts: 5.95 us -> 5.72 us
  transfers between devices with their start and end apart: 8 -> 8, of which waited for: 7 -> 6; matrix products, arithmetic and copies ran while one was open for 10% -> 12% of each run, Pallas kernels for 0% -> 0%
where the time goes in v1:
time: 245 us
  waiting for transfers between devices  132 us (54%)
  blocking collectives  31.5 us (13%)
  local copies, waits for them, and re-layouts  20.9 us (9%)
  matrix products  20.2 us (8%)
  other arithmetic  17.1 us (7%)
  between operations  14.9 us (6%)
  starting transfers between devices  8.59 us (4%)
    ppermute x3, waiting for transfers between devices, to_front(): return lax.ppermute(block, axis, [(i, i - 1) for i in range(1, n)])  60.5 us
    ppermute x3, waiting for transfers between devices, exchange(): return lax.ppermute(block, axis, [(i, partner(i, k, n)) for i in range(n)])  44.5 us
    all_to_all x1, blocking collectives, body(): lax.all_to_all(jnp.stack(jnp.split(new_weight, lax.axis_size('mp'), axis=...  31.5 us
    all_gather x1, waiting for transfers between devices, body(): weight_cols = lax.all_gather(weight_part, 'dp', axis=1, tiled=True)  26.6 us
    dot_general x1, matrix products, body(): lax.dot_general(activations, out_grad, (((0,), (0,)), ((), ())), preferre...  12.1 us
    broadcast_in_dim x2, local copies, waits for them, and re-layouts, mine(): return lax.dynamic_slice_in_dim(rows, begin, shard_rows, 0)[None]  11.4 us
    convert_element_type x3, other arithmetic, mine(): behind = to_front(block.astype(jnp.bfloat16), 'dp').astype(block.dtype)  8.67 us
    dot_general x1, matrix products, body(): jnp.dot(input_all, weight_cols, preferred_element_type=jnp.float32)  8.05 us
  transfers between devices with their start and end apart: 8, of which 6 were waited for; matrix products, arithmetic and copies ran while one was open for 12% of the time, Pallas kernels for 0%

profile of v1, /device:TPU:0, one launch (start us, length us, event | category | flops | bytes accessed | tf_op | source)
XLA Modules:
  0.0 244.8 jit_solution(1601410080283354524)
XLA Ops:
  7.2 1.0 copy-done
  8.2 12.1 %convolution_convert_fusion = bf16[256,8192]{1,0:T(8,128)(2,1)} fusion(bf16[1024,256]{1,0:T(8,128)(2,1)S(1)} %copy-done, bf16[1024,8192]{1,0:T(8,128)(2,1)} %param.8), kind=kOutput, calls=%fused_computation | convolution fusion | flops 4297064448 | bytes 21495808 | tf_op jit(solution)/shard_map/dot_general | solution.py:34
  20.3 3.6 %dynamic-slice_bitcast_fusion.2 = (bf16[64,8192]{1,0:T(8,128)(2,1)}, bf16[64,8192]{1,0:T(8,128)(2,1)}, bf16[64,8192]{1,0:T(8,128)(2,1)}) fusion(bf16[4,64,8192]{2,1,0:T(8,128)(2,1)} %bitcast.68, s32[]{:T(128)S(6)} %select_n.19, s32[]{:T(128)S(6)} %select_n.21, s32[]{:T(128)S(6)} %select_n.20), kind=kLoop, calls=%fused_computation.25 | loop fusion | bytes 6291468 | tf_op jit(solution)/shard_map/jit(dynamic_index_in_dim)/squeeze | solution.py:40
  23.9 3.9 %collective-permute-start.2 = (bf16[64,8192]{1,0:T(8,128)(2,1)}, bf16[64,8192]{1,0:T(8,128)(2,1)S(1)}, u32[]{:S(2)}, u32[]{:S(2)}) collective-permute-start(bf16[64,8192]{1,0:T(8,128)(2,1)} %get-tuple-element.15), channel_id=1, source_target_pairs={{0,24},{8,16},{16,8},{24,0},{1,25},{9,17},{17,9},{25,1},{2,26},{10... | collective-permute-start | bytes 3145736 | tf_op jit(solution)/shard_map/ppermute | solution.py:13
  29.2 22.9 %collective-permute-done.2 = bf16[64,8192]{1,0:T(8,128)(2,1)S(1)} collective-permute-done((bf16[64,8192]{1,0:T(8,128)(2,1)}, bf16[64,8192]{1,0:T(8,128)(2,1)S(1)}, u32[]{:S(2)}, u32[]{:S(2)}) %collective-permute-start.2) | collective-permute-done | bytes 1048608 | tf_op jit(solution)/shard_map/ppermute | solution.py:13
  52.1 21.6 %collective-permute-done.1 = bf16[64,8192]{1,0:T(8,128)(2,1)S(1)} collective-permute-done((bf16[64,8192]{1,0:T(8,128)(2,1)}, bf16[64,8192]{1,0:T(8,128)(2,1)S(1)}, u32[]{:S(2)}, u32[]{:S(2)}) %collective-permute-start.1) | collective-permute-done | bytes 1048608 | tf_op jit(solution)/shard_map/ppermute | solution.py:13
  74.6 5.9 %fusion.19 = (bf16[64,8192]{1,0:T(8,128)(2,1)}, f32[64,8192]{1,0:T(8,128)S(1)}, bf16[64,8192]{1,0:T(8,128)(2,1)}, f32[64,8192]{1,0:T(8,128)S(1)}) fusion(bf16[64,8192]{1,0:T(8,128)(2,1)} %copy-done.6, bf16[64,8192]{1,0:T(8,128)(2,1)} %copy-done.7, bf16[64,8192]{1,0:T(8,128)(2,1)} %collective-permute-done, bf16[4,64,8192]{2,1,0:T(8,128)(2,1)} %bitcast.69, ...), kind=kLoop, calls=%fused_computation.44 | loop fusion | flops 8388608 | bytes 14680068 | tf_op jit(solution)/shard_map/convert_element_type | solution.py:60
  80.6 1.1 fusion.7
  82.9 31.5 %all_to_all.5 = bf16[8,64,1024]{2,1,0:T(8,128)(2,1)} all-to-all(bf16[8,64,1024]{2,1,0:T(8,128)(2,1)S(1)} %fusion.11), channel_id=1, replica_groups=mesh['dp'=4,'mp'=8] {'mp'}, dimensions={0} | all-to-all | bytes 2097152 | tf_op jit(solution)/shard_map/all_to_all | solution.py:50
  114.4 1.3 collective-permute-start.5
  115.7 1.3 collective-permute-start.4
  117.2 1.5 collective-permute-start.3
  118.7 35.3 %collective-permute-done.5 = bf16[64,8192]{1,0:T(8,128)(2,1)} collective-permute-done((bf16[64,8192]{1,0:T(8,128)(2,1)}, bf16[64,8192]{1,0:T(8,128)(2,1)}, u32[]{:S(2)}, u32[]{:S(2)}) %collective-permute-start.5) | collective-permute-done | bytes 1048608 | tf_op jit(solution)/shard_map/ppermute | solution.py:23
  153.9 1.4 convert_element_type.62
  155.3 21.1 %collective-permute-done.4 = bf16[64,8192]{1,0:T(8,128)(2,1)} collective-permute-done((bf16[64,8192]{1,0:T(8,128)(2,1)}, bf16[64,8192]{1,0:T(8,128)(2,1)}, u32[]{:S(2)}, u32[]{:S(2)}) %collective-permute-start.4) | collective-permute-done | bytes 1048608 | tf_op jit(solution)/shard_map/ppermute | solution.py:23
  176.4 1.4 convert_element_type.60
  177.8 4.0 %fusion.1 = (f32[86,8192]{1,0:T(8,128)}, f32[86,8192]{1,0:T(8,128)}) fusion(s32[]{:T(128)S(6)} %select_n.22, f32[64,8192]{1,0:T(8,128)S(1)} %get-tuple-element.9, f32[64,8192]{1,0:T(8,128)S(1)} %convert_element_type.62, f32[86]{0:T(128)S(1)} %pad_dynamic-slice_fusion.6, f32[64,8192]{1,0:T(8,128)S(1)} %convert_element_type.60, f32[64,8192]{1,0:T(8,128)S(1)} %copy-done.3), kind=kLoop, calls=%fused_computation.9 | loop fusion | flops 2818048 | bytes 14025052 | tf_op jit(solution)/shard_map/concatenate | solution.py:61
  181.8 6.7 %broadcast_in_dim.14 = f32[1,86,8192]{2,0,1:T(1,128)} reshape(f32[86,8192]{1,0:T(8,128)} %get-tuple-element.18) | data formatting | bytes 5636096 | tf_op jit(solution)/shard_map/broadcast_in_dim | solution.py:62
  188.5 4.7 %broadcast_in_dim.15 = f32[1,86,8192]{2,0,1:T(1,128)} reshape(f32[86,8192]{1,0:T(8,128)S(1)} %copy-done.4) | data formatting | bytes 5636096 | tf_op jit(solution)/shard_map/broadcast_in_dim | solution.py:62
  193.2 4.1 %collective-permute-done.3 = bf16[64,8192]{1,0:T(8,128)(2,1)} collective-permute-done((bf16[64,8192]{1,0:T(8,128)(2,1)}, bf16[64,8192]{1,0:T(8,128)(2,1)}, u32[]{:S(2)}, u32[]{:S(2)}) %collective-permute-start.3) | collective-permute-done | bytes 1048608 | tf_op jit(solution)/shard_map/ppermute | solution.py:23
  197.3 3.4 %fusion.10 = bf16[1,86,8192]{2,1,0:T(8,128)(2,1)} fusion(s32[]{:T(128)S(6)} %select_n.22, bf16[64,8192]{1,0:T(8,128)(2,1)} %copy-done.5, bf16[64,8192]{1,0:T(8,128)(2,1)} %collective-permute-done.3, bf16[86]{0:T(256)(128)(2,1)S(1)} %pad_dynamic-slice_fusion.7), kind=kLoop, calls=%fused_computation.22 | loop fusion | flops 4227072 | bytes 3506352 | tf_op jit(solution)/shard_map/broadcast_in_dim | solution.py:62
  200.7 26.6 %all-gather.3.cloned.1.call-done = bf16[8,256,1024]{2,1,0:T(8,128)(2,1)} async-done(((bf16[8,64,1024]{2,1,0:T(8,128)(2,1)}), bf16[8,256,1024]{2,1,0:T(8,128)(2,1)}) %all-gather.3.cloned.1.call-update) | async-done | bytes 4194320 | tf_op jit(solution)/shard_map/all_gather | solution.py:55
  227.3 8.0 %convert_bitcast_fusion = bf16[1024,1024]{0,1:T(8,128)(2,1)S(1)} fusion(bf16[2048,1024]{1,0:T(8,128)(2,1)} %bitcast.70, bf16[1024,2048]{1,0:T(8,128)(2,1)} %all-gather.5.cloned.1.call-done), kind=kOutput, calls=%fused_computation.19 | convolution fusion | flops 4296015872 | bytes 10485760 | tf_op jit(solution)/shard_map/dot_general | solution.py:65
  235.4 2.6 %copy.11 = bf16[1024,1024]{1,0:T(8,128)(2,1)} copy(bf16[1024,1024]{0,1:T(8,128)(2,1)S(1)} %convert_bitcast_fusion) | data formatting | bytes 4194304
  (37 shorter events, 3.0 us)
Async XLA Ops:
  7.2 1.1 copy-start
  7.2 193.5 %all-gather.5.cloned.1.call-start = ((), (), s32[]{:S(2)}) async-start(), calls=%async_computation.2 | async-start | bytes 4718592 | tf_op jit(solution)/shard_map/all_gather | solution.py:33
  23.9 28.1 %collective-permute-start.2 = (bf16[64,8192]{1,0:T(8,128)(2,1)}, bf16[64,8192]{1,0:T(8,128)(2,1)S(1)}, u32[]{:S(2)}, u32[]{:S(2)}) collective-permute-start(bf16[64,8192]{1,0:T(8,128)(2,1)} %get-tuple-element.15), channel_id=1, source_target_pairs={{0,24},{8,16},{16,8},{24,0},{1,25},{9,17},{17,9},{25,1},{2,26},{10... | collective-permute-start | bytes 3145736 | tf_op jit(solution)/shard_map/ppermute | solution.py:13
  27.8 45.8 %collective-permute-start.1 = (bf16[64,8192]{1,0:T(8,128)(2,1)}, bf16[64,8192]{1,0:T(8,128)(2,1)S(1)}, u32[]{:S(2)}, u32[]{:S(2)}) collective-permute-start(bf16[64,8192]{1,0:T(8,128)(2,1)} %get-tuple-element.16), channel_id=1, source_target_pairs={{0,16},{8,24},{16,0},{24,8},{1,17},{9,25},{17,1},{25,9},{2,18},{10... | collective-permute-start | bytes 3145736 | tf_op jit(solution)/shard_map/ppermute | solution.py:13
  28.3 46.3 %collective-permute-start = (bf16[64,8192]{1,0:T(8,128)(2,1)}, bf16[64,8192]{1,0:T(8,128)(2,1)}, u32[]{:S(2)}, u32[]{:S(2)}) collective-permute-start(bf16[64,8192]{1,0:T(8,128)(2,1)} %get-tuple-element.14), channel_id=1, source_target_pairs={{0,8},{8,0},{16,24},{24,16},{1,9},{9,1},{17,25},{25,17},{2,10},{10... | collective-permute-start | bytes 3145736 | tf_op jit(solution)/shard_map/ppermute | solution.py:13
  28.4 198.9 %all-gather.3.cloned.1.call-start = ((), (), s32[]{:S(2)}) async-start(), calls=%async_computation.1 | async-start | bytes 5242880 | tf_op jit(solution)/shard_map/all_gather | solution.py:55
  29.2 51.4 %copy-start.8 = (bf16[1,64,8192]{2,1,0:T(8,128)(2,1)S(1)}, bf16[1,64,8192]{2,1,0:T(8,128)(2,1)}, u32[]{:S(2)}) copy-start(bf16[1,64,8192]{2,1,0:T(8,128)(2,1)} %param.9) | copy-start | bytes 3145732
  52.1 21.6 %copy-start.6 = (bf16[64,8192]{1,0:T(8,128)(2,1)}, bf16[64,8192]{1,0:T(8,128)(2,1)S(1)}, u32[]{:S(2)}) copy-start(bf16[64,8192]{1,0:T(8,128)(2,1)S(1)} %collective-permute-done.2) | copy-start | bytes 3145732
  73.6 1.0 copy-start.7
  80.6 1.3 copy-start.2
  81.9 1.0 copy-start.5
  114.4 39.5 %collective-permute-start.5 = (bf16[64,8192]{1,0:T(8,128)(2,1)}, bf16[64,8192]{1,0:T(8,128)(2,1)}, u32[]{:S(2)}, u32[]{:S(2)}) collective-permute-start(bf16[64,8192]{1,0:T(8,128)(2,1)} %get-tuple-element.8), channel_id=1, source_target_pairs={{8,0},{16,8},{24,16},{9,1},{17,9},{25,17},{10,2},{18,10},{26,18},{... | collective-permute-start | bytes 3145736 | tf_op jit(solution)/shard_map/ppermute | solution.py:23
  115.7 60.7 %collective-permute-start.4 = (bf16[64,8192]{1,0:T(8,128)(2,1)}, bf16[64,8192]{1,0:T(8,128)(2,1)}, u32[]{:S(2)}, u32[]{:S(2)}) collective-permute-start(bf16[64,8192]{1,0:T(8,128)(2,1)} %get-tuple-element.12), channel_id=1, source_target_pairs={{8,0},{16,8},{24,16},{9,1},{17,9},{25,17},{10,2},{18,10},{26,18},{... | collective-permute-start | bytes 3145736 | tf_op jit(solution)/shard_map/ppermute | solution.py:23
  117.2 80.1 %collective-permute-start.3 = (bf16[64,8192]{1,0:T(8,128)(2,1)}, bf16[64,8192]{1,0:T(8,128)(2,1)}, u32[]{:S(2)}, u32[]{:S(2)}) collective-permute-start(bf16[64,8192]{1,0:T(8,128)(2,1)} %copy-done.5), channel_id=1, source_target_pairs={{8,0},{16,8},{24,16},{9,1},{17,9},{25,17},{10,2},{18,10},{26,18},{... | collective-permute-start | bytes 3145736 | tf_op jit(solution)/shard_map/ppermute | solution.py:23
  155.3 22.5 %copy-start.3 = (f32[64,8192]{1,0:T(8,128)S(1)}, f32[64,8192]{1,0:T(8,128)}, u32[]{:S(2)}) copy-start(f32[64,8192]{1,0:T(8,128)} %copy-done.2) | copy-start | bytes 6291460
  181.8 6.7 %copy-start.4 = (f32[86,8192]{1,0:T(8,128)S(1)}, f32[86,8192]{1,0:T(8,128)}, u32[]{:S(2)}) copy-start(f32[86,8192]{1,0:T(8,128)} %get-tuple-element.17) | copy-start | bytes 8454148
  227.3 10.6 %copy-start.1 = (bf16[1024,256]{1,0:T(8,128)(2,1)S(1)}, bf16[1024,256]{1,0:T(8,128)(2,1)}, u32[]{:S(2)}) copy-start(bf16[1024,256]{1,0:T(8,128)(2,1)} %param.7) | copy-start | bytes 1572868
Sparse Core Ops, SparseCore 0:
  28.5 49.5 all-gather.4
  114.5 112.7 all-gather.2
